TPU v7x, 512 devices: a whole 4x8x8 slice. The times are simulated.
512 devices in a mesh: team: 64 (over z_hi, y, core), loop: 8 (over z_lo, x).
Axes of the slice: x: 4, y: 8, z: 8 (z_hi: 4, z_lo: 2; z = z_hi * 2 + z_lo), core: 2. Of those that a mesh axis runs over, the one named last changes fastest.
Arguments:
- src_pos: float32 [3, 262144], P(None, ('team', 'loop')), may hold values from -6 to 6
- src_vel: float32 [3, 262144], P(None, ('team', 'loop')), may hold values from -5 to 5
- src_mass: float32 [262144], P(('team', 'loop')), may hold values from 0.2 to 5
- old_accel: float32 [6, 8192], P(None, ('team', 'loop')), may hold values from -6 to 6
- active_index: int32 [8192], P(('team', 'loop')), may hold values from 0 to 511, as said below
- active_level: int32 [8192], P(('team', 'loop')), may hold values from 0 to 3
- tile_id: int32 [8192], P(('team', 'loop')), may hold values from 0 to 511
- tile_offset: int32 [2, 8192], P(None, ('team', 'loop')), may hold values from 16 to 112
Outputs:
- new_state: float32 [12, 8192], P(None, ('team', 'loop'))
- image: float32 [2, 512, 128, 128], P(None, ('team', 'loop'))
Inputs may be any that keep to these rules, and one draw needn't show every extreme that they name: `active_index`: the 16 entries of one device are distinct rows of that device's 512 source stars.
All inputs are finite; a program needn't handle non-finite values.
Results may differ from a plain program's by a relative error of at most 0.0027.
Values sent between devices are 32-bit elements; how exact they have to be, the bound alone decides.
A program may use at most 64 MiB of HBM per device.

v0:
```python
import math
import jax
import jax.numpy as jnp
from jax import lax
from jax.sharding import PartitionSpec as P

TILE_DEV = 1
TILE_W = 128


def from_behind(block, axis, distance):
    devices = range(lax.axis_size(axis))
    route = [((i - distance) % len(devices), i) for i in devices]
    return lax.ppermute(block, axis, route)


def pair_terms(tgt_pos, tgt_vel, blk_pos, blk_vel, blk_mass, gravity, soften_sq):
    separation = blk_pos[:, None, :] - tgt_pos[:, :, None]
    rel_vel = blk_vel[:, None, :] - tgt_vel[:, :, None]
    dist_sq = jnp.sum(separation * separation, axis=0) + soften_sq
    inverse = lax.rsqrt(dist_sq)
    inverse_sq = inverse * inverse
    strength = (gravity * blk_mass)[None, :] * inverse * inverse_sq
    radial = 3.0 * jnp.sum(separation * rel_vel, axis=0) * inverse_sq
    acceleration = jnp.sum(strength[None] * separation, axis=2)
    jerk_sum = jnp.sum(strength[None] * (rel_vel - radial[None] * separation), axis=2)
    return jnp.concatenate([acceleration, jerk_sum], axis=0)


def correct(targets, force, old_accel, level_float):
    step_len = jnp.exp2(-level_float)
    accel_gap = old_accel[0:3] - force[0:3]
    first_term = -6.0 * accel_gap - step_len * (4.0 * old_accel[3:6] + 2.0 * force[3:6])
    second = 12.0 * accel_gap + 6.0 * step_len * (old_accel[3:6] + force[3:6])
    new_pos = targets[0:3] + step_len * step_len * (first_term / 24.0 + second / 120.0)
    new_vel = targets[3:6] + step_len * (first_term / 6.0 + second / 24.0)
    return jnp.concatenate([new_pos, new_vel, force], axis=0)


def ingredients(new_state, star_mass, offsets, width):
    swing_cells = width / 16.0
    centre_y = offsets[0] + swing_cells * jnp.tanh(new_state[1])
    centre_x = offsets[1] + swing_cells * jnp.tanh(new_state[0])
    return jnp.stack([star_mass, star_mass * new_state[5] * new_state[5], centre_y, centre_x])


def kernel_rows(centre, width):
    cell_mid = jnp.arange(width, dtype=jnp.float32) + 0.5
    scaled = (cell_mid[None, :] - centre[:, None]) / (width / 40.0)
    return jnp.exp(-0.5 * scaled * scaled)


def block_forces(targets, source, gravity, soften_sq):
    source_len = source.shape[1]
    block_len = math.gcd(source_len, 512)
    blocks = source.reshape(7, source_len // block_len, block_len).transpose(1, 0, 2)

    def add_block(running, block_now):
        return (
            running
            + pair_terms(
                targets[0:3],
                targets[3:6],
                block_now[0:3],
                block_now[3:6],
                block_now[6],
                gravity,
                soften_sq,
            ),
            None,
        )

    return lax.scan(add_block, jnp.zeros((6, targets.shape[1]), jnp.float32), blocks)[0]


def shards(src_pos, src_vel, src_mass, old_accel, active_index, active_level, tile_id, tile_offset):
    total_stars = src_pos.shape[1] * lax.axis_size("team") * lax.axis_size("loop")
    gravity = 1.0 / total_stars
    soften_sq = float(total_stars) ** (-2.0 / 3.0)
    own_records = jnp.concatenate(
        [jnp.take(src_pos, active_index, axis=1), jnp.take(src_vel, active_index, axis=1)], axis=0
    )
    own_mass = jnp.take(src_mass, active_index, axis=0)
    source = jnp.concatenate([src_pos, src_vel, src_mass[None]], axis=0)
    owned_tiles = lax.axis_index(("team", "loop")) * TILE_DEV + jnp.arange(
        TILE_DEV, dtype=jnp.int32
    )
    empty_image = jnp.zeros((2, TILE_DEV, TILE_W, TILE_W), jnp.float32)
    targets = lax.all_gather(own_records, "team", axis=1, tiled=True)
    total_force = block_forces(targets, source, gravity, soften_sq)
    moving = source
    for turn in range(lax.axis_size("loop") - 1):
        moving = from_behind(moving, "loop", 1)
        total_force = total_force + block_forces(targets, moving, gravity, soften_sq)
    own_force = lax.psum_scatter(total_force, "team", scatter_dimension=1, tiled=True)
    new_state = correct(own_records, own_force, old_accel, active_level.astype(jnp.float32))
    deposit_parts = ingredients(new_state, own_mass, tile_offset.astype(jnp.float32), TILE_W)
    deposit_deposit_parts = lax.all_gather(deposit_parts, ("team", "loop"), axis=1, tiled=True)
    tile_rows = lax.all_gather(tile_id[None], ("team", "loop"), axis=1, tiled=True)
    row_count = deposit_deposit_parts.shape[1]
    star_block = math.gcd(row_count, 256)
    order = jnp.argsort(tile_rows[0], stable=True)
    sorted_tiles = jnp.take(tile_rows[0], order, axis=0)
    sorted_parts = jnp.take(deposit_deposit_parts, order, axis=1)
    low_row = jnp.sum((sorted_tiles < owned_tiles[0]).astype(jnp.int32))
    high_row = jnp.sum((sorted_tiles <= owned_tiles[TILE_DEV - 1]).astype(jnp.int32))
    first_block = low_row // star_block
    end_block = (high_row + star_block - 1) // star_block

    def add_stars(block_idx, running):
        first_row = block_idx * star_block
        part_block = lax.dynamic_slice_in_dim(sorted_parts, first_row, star_block, 1)
        tile_block = lax.dynamic_slice_in_dim(sorted_tiles, first_row, star_block, 0)
        tile_mask = (tile_block[None, :] == owned_tiles[:, None]).astype(jnp.float32)
        weighted = part_block[0:2, :, None] * kernel_rows(part_block[2], TILE_W)[None]
        left_rows = (weighted[:, None] * tile_mask[None, :, :, None]).astype(jnp.bfloat16)
        right_rows = kernel_rows(part_block[3], TILE_W).astype(jnp.bfloat16)
        return running + jnp.einsum(
            "ltsy,sx->ltyx", left_rows, right_rows, preferred_element_type=jnp.float32
        )

    image = lax.fori_loop(first_block, end_block, add_stars, empty_image)
    return (new_state, image)


def solution(mesh):
    return jax.shard_map(
        shards,
        mesh=mesh,
        in_specs=(
            P(None, ("team", "loop")),
            P(None, ("team", "loop")),
            P(("team", "loop")),
            P(None, ("team", "loop")),
            P(("team", "loop")),
            P(("team", "loop")),
            P(("team", "loop")),
            P(None, ("team", "loop")),
        ),
        out_specs=(P(None, ("team", "loop")), P(None, ("team", "loop"), None, None)),
        check_vma=False,
    )
```

profile of v0, /device:TPU:2, one launch (start us, length us, event | category | flops | bytes accessed | tf_op | source)
XLA Modules:
  0.0 1785.6 jit_solution(9198500476613658640)
XLA Ops:
  7.2 0.7 pad_maximum_fusion
  8.0 3.4 collective-permute-start
  11.4 0.8 copy.89
  12.2 0.8 copy.91
  13.1 0.7 compare_select_fusion.1
  13.7 0.7 compare_and_fusion.1
  15.7 89.0 %all-gather.1 = f32[64,16,6]{1,2,0:T(8,128)S(1)} all-gather(f32[1,16,6]{1,2,0:T(8,128)S(1)} %maximum_bitcast_fusion), channel_id=1, replica_groups=mesh['team'=64,'loop'=8] {'team'}, dimensions={0}, use_global_device_ids=true | all-gather | bytes 24960 | tf_op jit(solution)/shard_map/all_gather | solution.py:89
  104.9 0.9 dynamic-update-slice
  105.7 95.0 %all-reduce = s32[8192]{0:T(1024)S(1)} all-reduce(s32[8192]{0:T(1024)S(1)} %dynamic-update-slice), channel_id=2, replica_groups=mesh['team'=64,'loop'=8] {'team','loop'}, use_global_device_ids=true, to_apply=%add | all-reduce | flops 8192 | bytes 65536
  200.8 6.8 sort.17
  207.6 45.5 %gather_fusion = s32[8192]{0:T(1024)S(1)} fusion(s32[8192]{0:T(1024)S(1)} %all-reduce, s32[8192]{0:T(1024)S(1)} %fusion.63), kind=kCustom, calls=%fused_computation.2 | custom fusion | bytes 98304 | tf_op jit(solution)/shard_map/jit(_take)/gather | solution.py:103
  253.1 0.6 convert_reduce_fusion
  253.8 2.1 collective-permute-start.1
  255.9 3.5 collective-permute-done.1
  259.4 1.8 fusion.39
  261.2 2.1 collective-permute-start.2
  263.3 0.7 multiply_multiply_fusion.10
  264.0 4.3 collective-permute-done.2
  268.3 1.9 collective-permute-start.3
  270.3 5.8 collective-permute-done.3
  276.1 8.1 fusion.40
  284.2 1.6 multiply_multiply_fusion.7
  285.8 2.1 collective-permute-start.4
  288.0 2.6 multiply_multiply_fusion.14
  290.6 3.0 collective-permute-done.4
  293.6 1.9 collective-permute-start.5
  295.5 5.8 collective-permute-done.5
  301.3 1.9 collective-permute-start.6
  303.3 5.8 collective-permute-done.6
  309.1 14.1 fusion.37
  323.2 3.0 multiply_multiply_fusion.8
  326.1 3.0 fusion.43
  329.1 0.7 multiply_multiply_fusion.5
  329.8 0.7 multiply_multiply_fusion.3
  330.5 0.7 multiply_multiply_fusion.1
  331.2 0.9 copy-done.1
  332.7 10.1 fusion.34
  342.9 1.0 copy.97
  344.0 0.7 gather_fusion.1
  347.7 139.5 %reduce-scatter.4.cloned.1.call-done = f32[16,6]{1,0:T(8,128)} async-done(((f32[1024,6]{1,0:T(8,128)}), f32[16,6]{1,0:T(8,128)}) %reduce-scatter.4.cloned.1.call-update) | async-done | bytes 400
  487.2 0.8 copy.98
  488.7 1244.0 %all-gather.2 = f32[512,16,4]{1,2,0:T(4,128)S(1)} all-gather(f32[1,16,4]{1,2,0:T(4,128)S(1)} %maximum_bitcast_fusion.1), channel_id=1, replica_groups=mesh['team'=64,'loop'=8] {'team','loop'}, dimensions={0}, use_global_device_ids=true | all-gather | bytes 131328 | tf_op jit(solution)/shard_map/all_gather | solution.py:98
  1732.6 4.5 copy.94
  1737.1 29.9 %gather_fusion.2 = f32[8192,4]{1,0:T(8,128)} fusion(f32[4,8192]{0,1:T(8,128)} %bitcast.52, s32[8192]{0:T(1024)S(1)} %fusion.63), kind=kCustom, calls=%fused_computation.4 | custom fusion | bytes 294912 | tf_op jit(solution)/shard_map/jit(_take)/gather | solution.py:104
  1767.0 7.4 select_bitcast_fusion
  1774.5 2.8 copy.95
  1777.3 0.7 while.9
  1778.1 0.6 copy-done.5
  (66 shorter events, 3.7 us)
Async XLA Ops:
  7.2 480.0 %reduce-scatter.4.cloned.1.call-start = ((), (), s32[]{:S(2)}) async-start(), calls=%async_computation.1 | async-start | bytes 532480
  8.0 245.8 %collective-permute-start = (f32[7,512]{1,0:T(8,128)S(1)}, f32[7,512]{1,0:T(8,128)S(1)}, u32[]{:S(2)}, u32[]{:S(2)}) collective-permute-start(f32[7,512]{1,0:T(8,128)S(1)} %pad_maximum_fusion), channel_id=1, source_target_pairs={{7,0},{0,1},{1,2},{2,3},{3,4},{4,5},{5,6},{6,7},{15,8},{8,9},{9,10... | collective-permute-start | bytes 43016 | tf_op jit(solution)/shard_map/ppermute | solution.py:14
  207.6 46.2 %copy-start = (f32[512]{0:T(512)S(1)}, f32[512]{0:T(512)}, u32[]{:S(2)}) copy-start(f32[512]{0:T(512)} %param.14) | copy-start | bytes 6148
  253.8 5.6 collective-permute-start.1
  261.2 7.1 collective-permute-start.2
  263.3 12.8 copy-start.3
  263.3 12.8 copy-start.4
  268.3 7.7 collective-permute-start.3
  285.8 7.7 collective-permute-start.4
  293.6 7.7 collective-permute-start.5
  301.3 7.7 collective-permute-start.6
  330.5 1.6 copy-start.1
  330.5 2.2 copy-start.2
  332.7 11.3 copy-start.9
  332.7 14.9 copy-start.7
  332.7 155.2 %copy-start.6 = (f32[6,16]{1,0:T(8,128)S(1)}, f32[6,16]{1,0:T(8,128)}, u32[]{:S(2)}) copy-start(f32[6,16]{1,0:T(8,128)} %param.15) | copy-start | bytes 1156
  332.7 155.3 %copy-start.8 = (s32[16]{0:T(128)S(1)}, s32[16]{0:T(128)}, u32[]{:S(2)}) copy-start(s32[16]{0:T(128)} %param.16) | copy-start | bytes 196
  1778.1 0.7 copy-start.5
Sparse Core Ops, SparseCore 0:
  344.1 143.0 reduce-scatter.3
where the time goes:
time: 1790 us
  blocking collectives  1430 us (80%)
  waiting for transfers between devices  168 us (9%)
  local copies, waits for them, and re-layouts  91.7 us (5%)
  other arithmetic  65 us (4%)
    all_gather x1, blocking collectives, shards(): lax.all_gather(deposit_parts, ('team', 'loop'), axis=1, tiled=True)  1240 us
    unnamed x2, waiting for transfers between devices  140 us
    unnamed x1, blocking collectives  95 us
    all_gather x1, blocking collectives, shards(): targets = lax.all_gather(own_records, 'team', axis=1, tiled=True)  89 us
    gather x1, local copies, waits for them, and re-layouts, shards(): sorted_tiles = jnp.take(tile_rows[0], order, axis=0)  45.5 us
  transfers between devices with their start and end apart: 8, of which 7 were waited for; matrix products, arithmetic and copies ran while one was open for 3% of the time, Pallas kernels for 0%

commit v1 on v0

--- a/solution.py
+++ b/solution.py
@@ -86,7 +86,8 @@
         TILE_DEV, dtype=jnp.int32
     )
     empty_image = jnp.zeros((2, TILE_DEV, TILE_W, TILE_W), jnp.float32)
-    targets = lax.all_gather(own_records, "team", axis=1, tiled=True)
+    sent = jnp.stack([own_records] * lax.axis_size("team"))
+    targets = jnp.concatenate(lax.all_to_all(sent, "team", 0, 0), axis=1)
     total_force = block_forces(targets, source, gravity, soften_sq)
     moving = source
     for turn in range(lax.axis_size("loop") - 1):

time: 1790 us -> 1720 us (0.961)
  blocking collectives: 1430 us -> 1340 us
  starting transfers between devices: 15.4 us -> 33.4 us
    all_gather x1 -> x0, blocking collectives: 89 us -> none  [shards(): targets = lax.all_gather(own_records, 'team', axis=1, tiled=True)]
  transfers between devices with their start and end apart: 8 -> 9, of which waited for: 7 -> 7; matrix products, arithmetic and copies ran while one was open for 3% -> 4% of each run, Pallas kernels for 0% -> 0%
where the time goes in v1:
time: 1720 us
  blocking collectives  1340 us (78%)
  waiting for transfers between devices  167 us (10%)
  local copies, waits for them, and re-layouts  92.5 us (5%)
  other arithmetic  68.9 us (4%)
  starting transfers between devices  33.4 us (2%)
  between operations  17.5 us (1%)
    all_gather x1, blocking collectives, shards(): lax.all_gather(deposit_parts, ('team', 'loop'), axis=1, tiled=True)  1240 us
    unnamed x2, waiting for transfers between devices  144 us
    unnamed x1, blocking collectives  98.5 us
    gather x1, local copies, waits for them, and re-layouts, shards(): sorted_tiles = jnp.take(tile_rows[0], order, axis=0)  45.5 us
    reduce_sum x4, other arithmetic, pair_terms(): acceleration = jnp.sum(strength[None] * separation, axis=2)  37.5 us
  transfers between devices with their start and end apart: 9, of which 7 were waited for; matrix products, arithmetic and copies ran while one was open for 4% of the time, Pallas kernels for 0%

profile of v1, /device:TPU:2, one launch (start us, length us, event | category | flops | bytes accessed | tf_op | source)
XLA Modules:
  0.0 1722.6 jit_solution(12391863718480742441)
XLA Ops:
  7.2 0.7 compare_select_fusion.1
  7.8 0.7 compare_and_fusion.1
  8.5 0.8 copy.91
  10.0 0.8 copy.93
  11.5 0.7 stack.4
  12.2 16.6 all-to-all-start
  28.8 0.7 pad_maximum_fusion
  29.6 3.4 collective-permute-start
  33.0 0.9 dynamic-update-slice
  33.9 98.5 %all-reduce = s32[8192]{0:T(1024)S(1)} all-reduce(s32[8192]{0:T(1024)S(1)} %dynamic-update-slice), channel_id=2, replica_groups=mesh['team'=64,'loop'=8] {'team','loop'}, use_global_device_ids=true, to_apply=%add | all-reduce | flops 8192 | bytes 65536
  132.4 6.8 sort.17
  139.2 45.5 %gather_fusion = s32[8192]{0:T(1024)S(1)} fusion(s32[8192]{0:T(1024)S(1)} %all-reduce, s32[8192]{0:T(1024)S(1)} %fusion.63), kind=kCustom, calls=%fused_computation.2 | custom fusion | bytes 98304 | tf_op jit(solution)/shard_map/jit(_take)/gather | solution.py:104
  184.8 0.6 convert_reduce_fusion
  185.4 1.9 collective-permute-start.1
  187.4 3.7 collective-permute-done.1
  191.1 1.9 collective-permute-start.2
  193.0 4.3 collective-permute-done.2
  197.2 2.1 collective-permute-start.3
  199.7 1.8 fusion.39
  201.5 0.7 multiply_multiply_fusion.10
  202.2 2.8 collective-permute-done.3
  205.0 10.2 fusion.40
  215.2 3.6 multiply_multiply_fusion.7
  218.8 2.0 collective-permute-start.4
  220.8 2.6 multiply_multiply_fusion.14
  223.5 3.1 collective-permute-done.4
  226.5 3.2 collective-permute-start.5
  229.8 4.4 collective-permute-done.5
  234.2 2.1 collective-permute-start.6
  236.4 5.6 collective-permute-done.6
  242.0 14.9 fusion.37
  256.9 3.0 multiply_multiply_fusion.8
  259.9 2.6 fusion.43
  262.5 0.7 multiply_multiply_fusion.5
  263.8 0.7 multiply_multiply_fusion.1
  264.4 0.9 copy-done.1
  266.0 9.7 fusion.34
  275.8 1.0 copy.100
  276.8 0.7 gather_fusion.1
  280.5 143.7 %reduce-scatter.4.cloned.1.call-done = f32[16,6]{1,0:T(8,128)} async-done(((f32[1024,6]{1,0:T(8,128)}), f32[16,6]{1,0:T(8,128)}) %reduce-scatter.4.cloned.1.call-update) | async-done | bytes 400
  424.2 0.8 copy.101
  425.6 1244.0 %all-gather.1 = f32[512,16,4]{1,2,0:T(4,128)S(1)} all-gather(f32[1,16,4]{1,2,0:T(4,128)S(1)} %maximum_bitcast_fusion), channel_id=1, replica_groups=mesh['team'=64,'loop'=8] {'team','loop'}, dimensions={0}, use_global_device_ids=true | all-gather | bytes 131328 | tf_op jit(solution)/shard_map/all_gather | solution.py:99
  1669.7 4.5 copy.97
  1674.2 29.9 %gather_fusion.2 = f32[8192,4]{1,0:T(8,128)} fusion(f32[4,8192]{0,1:T(8,128)} %bitcast.46, s32[8192]{0:T(1024)S(1)} %fusion.63), kind=kCustom, calls=%fused_computation.4 | custom fusion | bytes 294912 | tf_op jit(solution)/shard_map/jit(_take)/gather | solution.py:105
  1704.1 7.5 select_bitcast_fusion
  1711.5 2.8 copy.98
  1714.4 0.7 while.9
  1715.1 0.6 copy-done.5
  (70 shorter events, 4.4 us)
Async XLA Ops:
  12.2 187.2 %all-to-all-start = ((f32[64,6,16]{2,1,0:T(8,128)}), f32[64,6,16]{2,1,0:T(8,128)S(1)}, u32[]{:S(2)}, u32[]{:S(2)}) async-start(f32[64,6,16]{2,1,0:T(8,128)} %stack.4), calls=%async_computation | async-start | bytes 524288 | tf_op jit(solution)/shard_map/all_to_all | solution.py:90
  28.8 395.4 %reduce-scatter.4.cloned.1.call-start = ((), (), s32[]{:S(2)}) async-start(), calls=%async_computation.2 | async-start | bytes 532480
  29.6 155.8 %collective-permute-start = (f32[7,512]{1,0:T(8,128)S(1)}, f32[7,512]{1,0:T(8,128)S(1)}, u32[]{:S(2)}, u32[]{:S(2)}) collective-permute-start(f32[7,512]{1,0:T(8,128)S(1)} %pad_maximum_fusion), channel_id=1, source_target_pairs={{7,0},{0,1},{1,2},{2,3},{3,4},{4,5},{5,6},{6,7},{15,8},{8,9},{9,10... | collective-permute-start | bytes 43016 | tf_op jit(solution)/shard_map/ppermute | solution.py:14
  139.2 46.2 %copy-start = (f32[512]{0:T(512)S(1)}, f32[512]{0:T(512)}, u32[]{:S(2)}) copy-start(f32[512]{0:T(512)} %param.14) | copy-start | bytes 6148
  185.4 5.6 collective-permute-start.1
  191.1 6.2 collective-permute-start.2
  197.2 7.7 collective-permute-start.3
  201.5 3.5 copy-start.3
  201.5 3.5 copy-start.4
  218.8 7.7 collective-permute-start.4
  226.5 7.7 collective-permute-start.5
  234.2 7.7 collective-permute-start.6
  263.7 1.6 copy-start.1
  263.8 2.2 copy-start.2
  266.0 10.8 copy-start.9
  266.0 14.5 copy-start.7
  266.0 159.0 %copy-start.6 = (f32[6,16]{1,0:T(8,128)S(1)}, f32[6,16]{1,0:T(8,128)}, u32[]{:S(2)}) copy-start(f32[6,16]{1,0:T(8,128)} %param.15) | copy-start | bytes 1156
  266.0 159.0 %copy-start.8 = (s32[16]{0:T(128)S(1)}, s32[16]{0:T(128)}, u32[]{:S(2)}) copy-start(s32[16]{0:T(128)} %param.16) | copy-start | bytes 196
  1715.1 0.7 copy-start.5
Sparse Core Ops, SparseCore 0:
  276.9 147.1 reduce-scatter.3
